TPU v7x, 512 devices: a whole 4x4x16 slice. The times are simulated.
512 devices in a mesh: sub: 32 (over x_lo, z), beam: 16 (over x_hi, y, core).
Axes of the slice: x: 4 (x_hi: 2, x_lo: 2; x = x_hi * 2 + x_lo), y: 4, z: 16, core: 2. Of those that a mesh axis runs over, the one named last changes fastest.
Arguments:
- echoes: bfloat16 [64, 32, 2, 16384], P('sub', 'beam'), may hold values from -6 to 6
- matched_filter: float32 [2, 16384], replicated, may hold values from -6 to 6
- steering: bfloat16 [2, 128, 32], P(None, 'beam'), may hold values from -1 to 1
- kernels: bfloat16 [4, 2, 2, 128, 128], replicated, may hold values from -0.375 to 0.375
- blend_gains: float32 [4, 2, 2, 2], replicated, may hold values from 0.3 to 1
- beam_taps: int32 [4, 2, 2, 128], P(None, None, None, 'beam'), may hold values from -1 to 0
Outputs:
- polar_image: bfloat16 [64, 128, 2, 16384], P('sub', 'beam')
Inputs may be any that keep to these rules, and one draw needn't show every extreme that they name: `beam_taps`: a parent row n reads child rows n + t and n + t + 1.
All inputs are finite; a program needn't handle non-finite values.
Results may differ from a plain program's by a relative error of at most 0.019.
Values may be sent and summed in bfloat16 or wider, within the bound.
No kernel may reach another device: no remote copies, remote signals or barrier semaphores. Data moves between devices by JAX's collectives and lax.ppermute only.
A program may use at most 64 MiB of HBM per device.

v0:
```python
import math
import jax
import jax.numpy as jnp
import numpy as np
from jax import lax
from jax.sharding import Mesh
from jax.sharding import PartitionSpec as P

FA = 128
LEVELS = 4
HIGH = lax.Precision.HIGH


def table_product(form, left, right):
    return jnp.einsum(form, left, right, precision=HIGH)


def dft_tables(order, sign, modulus):
    index = np.arange(order)
    phase = index[:, None] * index[None, :] % modulus
    angle = phase * (sign * 2.0 * math.pi / modulus)
    return (jnp.asarray(np.cos(angle), jnp.float32), jnp.asarray(np.sin(angle), jnp.float32))


def four_step(real_part, imag_part, sign):
    order = real_part.shape[-1]
    cos_small, sin_small = dft_tables(order, sign, order)
    cos_turn, sin_turn = dft_tables(order, sign, order * order)
    first_real = table_product("kn,qnm->qkm", cos_small, real_part) - table_product(
        "kn,qnm->qkm", sin_small, imag_part
    )
    first_imag = table_product("kn,qnm->qkm", cos_small, imag_part) + table_product(
        "kn,qnm->qkm", sin_small, real_part
    )
    turned_real = first_real * cos_turn - first_imag * sin_turn
    turned_imag = first_real * sin_turn + first_imag * cos_turn
    out_real = table_product("qkm,mj->qjk", turned_real, cos_small) - table_product(
        "qkm,mj->qjk", turned_imag, sin_small
    )
    out_imag = table_product("qkm,mj->qjk", turned_real, sin_small) + table_product(
        "qkm,mj->qjk", turned_imag, cos_small
    )
    return (out_real, out_imag)


def compress(echoes, matched_filter):
    count = echoes.shape[0] * echoes.shape[1]
    length = echoes.shape[-1]
    signal = echoes.astype(jnp.float32).reshape(count, 2, FA, FA)
    spec_real, spec_imag = four_step(signal[:, 0], signal[:, 1], -1.0)
    matched = matched_filter.reshape(2, FA, FA)
    prod_real = spec_real * matched[0] - spec_imag * matched[1]
    prod_imag = spec_real * matched[1] + spec_imag * matched[0]
    back_real, back_imag = four_step(prod_real, prod_imag, 1.0)
    stacked = jnp.stack([back_real, back_imag], axis=1) / length
    return stacked.reshape(echoes.shape[:3] + (FA, FA)).astype(jnp.bfloat16)


def as_blocks(pair):
    real_part, imag_part = (pair[..., 0, :, :], pair[..., 1, :, :])
    top = jnp.concatenate([real_part, imag_part], axis=-1)
    bottom = jnp.concatenate([-imag_part, real_part], axis=-1)
    return jnp.concatenate([top, bottom], axis=-2)


def pick(table, index):
    return lax.dynamic_index_in_dim(table, index, 0, keepdims=False)


def range_chain(kernels, bits):
    blocks = as_blocks(kernels.astype(jnp.float32))
    chain = pick(blocks[3], bits[2])
    chain = table_product("ik,kj->ij", pick(blocks[2], bits[1]), chain)
    chain = table_product("ik,kj->ij", pick(blocks[1], bits[0]), chain)
    return table_product("cik,kj->cij", blocks[0], chain).astype(jnp.bfloat16)


def band_matrices(taps, gains):
    rows = taps.shape[0]
    first = jnp.moveaxis(taps, 0, -1).astype(jnp.int32)[..., None] + jnp.arange(rows)[:, None]
    column = jnp.arange(rows)
    lower = jnp.where(column == first, gains[..., 0, None, None], 0.0)
    upper = jnp.where(column == first + 1, gains[..., 1, None, None], 0.0)
    return lower + upper


def local(echoes, matched_filter, steering, kernels, blend_gains, beam_taps):
    zh = lax.axis_index("zh")
    zl = lax.axis_index("zl")
    own_rows = steering.shape[1]
    pulses = steering.shape[2]
    own_pulses = echoes.shape[1]
    beams = pulses // own_pulses
    packed = jnp.concatenate(
        [
            jnp.moveaxis(steering, 1, 0).reshape(own_rows, 2 * pulses),
            jnp.moveaxis(beam_taps, 3, 0).reshape(own_rows, 4 * LEVELS).astype(jnp.bfloat16),
        ],
        axis=1,
    )
    packed = jnp.pad(packed, ((0, 0), (0, 128 - packed.shape[1])))
    packed = lax.all_gather(packed, "beam", axis=0, tiled=True)
    rows = packed.shape[0]
    compressed = compress(echoes, matched_filter)
    mats = range_chain(kernels, (zl & 1, zl >> 1, zh)).reshape(2, 2, FA, 2, FA)
    turned = jnp.einsum(
        "spinm,simoj->sponj", compressed, mats, preferred_element_type=jnp.float32
    ).astype(jnp.bfloat16)
    width = 2 * own_pulses * 2
    peers = 4 * beams
    message = jnp.moveaxis(turned.reshape(width, peers, -1), 1, 0)
    own = lax.all_to_all(message, ("zl", "beam"), 0, 0, tiled=True).reshape(peers * width, -1)
    other = lax.ppermute(own, "zh", [(0, 1), (1, 0)])
    steer = packed[:, : 2 * pulses].astype(jnp.float32).reshape(rows, 2, beams, own_pulses)
    taps = packed[:, 2 * pulses : 2 * pulses + 4 * LEVELS].reshape(rows, LEVELS, 2, 2)
    band = band_matrices(taps, blend_gains)
    mixing = jnp.stack(
        [jnp.stack([steer[:, 0], -steer[:, 1]], -1), jnp.stack([steer[:, 1], steer[:, 0]], -1)], 1
    )
    lead = table_product("cenm,mobpi->enobcpi", band[0], mixing).reshape(2, rows, -1)
    lead = table_product("cenm,fmx->cefnx", band[1], lead)
    lead = table_product("cenm,dfgmx->cdefgnx", band[2], lead)

    def last(child):
        b4 = pick(pick(band[3], child), zh)
        full = table_product("nm,cdefgmx->cdefgnx", b4, lead).astype(jnp.bfloat16)
        full = full.reshape(2, 2, 2, 2, 2, beams, own_rows, 2, FA)
        full = jnp.transpose(full, (2, 3, 5, 4, 7, 6, 0, 1, 8))
        return full.reshape(4 * beams * 2 * 2 * own_rows, 4 * FA)

    total = jnp.dot(last(zh), own, preferred_element_type=jnp.float32)
    total = total + jnp.dot(last(1 - zh), other, preferred_element_type=jnp.float32)
    result = total.astype(jnp.bfloat16).reshape(peers, 2 * 2 * own_rows, -1)
    arrived = lax.all_to_all(result, ("zl", "beam"), 0, 0, tiled=True)
    arrived = arrived.reshape(peers, 2, 2, own_rows, -1)
    return jnp.transpose(arrived, (1, 3, 2, 0, 4)).reshape(2, own_rows, 2, -1)


def solution(mesh):
    fine = Mesh(mesh.devices.reshape(4, 2, 4, 16), ("g", "zh", "zl", "beam"))
    sub = ("g", "zh", "zl")
    return jax.shard_map(
        local,
        mesh=fine,
        in_specs=(
            P(sub, "beam", None, None),
            P(),
            P(None, "beam", None),
            P(),
            P(),
            P(None, None, None, "beam"),
        ),
        out_specs=P(sub, "beam", None, None),
        check_vma=False,
    )
```

profile of v0, /device:TPU:1, one launch (start us, length us, event | category | flops | bytes accessed | tf_op | source)
XLA Modules:
  0.0 150.1 jit_solution(6426579035786599615)
XLA Ops:
  0.0 1.2 reshape.128
  1.2 1.1 fusion.34
  2.3 1.1 fusion.33
  3.4 1.1 convolution_add_fusion.4
  4.4 0.2 convolution_subtract_fusion.3
  4.7 0.3 fusion.20
  5.0 0.3 fusion.22
  5.2 0.3 fusion.13
  5.5 0.3 fusion.14
  6.1 0.3 fusion.43
  6.4 0.3 fusion.44
  6.7 0.3 fusion.12
  7.0 0.3 fusion.11
  7.3 0.4 fusion.36
  7.7 0.4 fusion.35
  8.2 0.9 slice_bitcast_fusion.2
  9.2 0.4 convolution_subtract_fusion
  9.7 0.4 convolution_add_fusion.1
  10.1 0.8 copy.172
  10.9 1.4 maximum_maximum_fusion
  12.3 1.0 fusion.59
  13.3 0.3 fusion.25
  13.6 1.3 convolution_bitcast_fusion.3
  14.8 0.4 convolution_convert_fusion
  15.3 0.3 fusion.10
  15.6 0.2 copy.174
  15.9 0.9 copy.175
  16.8 13.1 %all-to-all-start = ((bf16[64,8,256]{2,1,0:T(8,128)(2,1)}), bf16[64,8,256]{2,1,0:T(8,128)(2,1)S(1)}, u32[]{:S(2)}, u32[]{:S(2)}) async-start(bf16[64,8,256]{2,1,0:T(8,128)(2,1)} %copy.175), calls=%async_computation | async-start | bytes 524288 | tf_op jit(solution)/shard_map/all_to_all | solution.py:112
  30.1 24.7 %all_gather.3 = bf16[128,128]{1,0:T(8,128)(2,1)S(1)} all-gather(bf16[8,128]{1,0:T(8,128)(2,1)S(1)} %fusion.47), channel_id=1, replica_groups=mesh['g'=4,'zh'=2,'zl'=4,'beam'=16] {'beam'}, dimensions={0}, use_global_device_ids=true | all-gather | bytes 34816 | tf_op jit(solution)/shard_map/all_gather | solution.py:102
  55.3 0.6 select_add_fusion
  56.0 0.3 convolution_bitcast_fusion.4
  56.3 0.2 copy.158
  56.5 0.6 convolution_bitcast_fusion.1
  57.1 1.9 %convolution_bitcast_fusion = f32[2,2,2,2,2,128,256]{5,6,2,0,4,3,1:T(8,128)S(1)} fusion(f32[2,2,2,128,256,1,1]{3,4,6,5,2,1,0:T(8,128)S(1)} %convolution_bitcast_fusion.1, f32[4,2,2,128,128]{4,3,2,1,0:T(8,128)S(1)} %select_add_fusion), kind=kOutput, calls=%fused_computation.6 | convolution fusion | flops 805306368 | bytes 5505024 | tf_op jit(solution)/shard_map/cenm,dfgmx->cdefgnx/dot_general | solution.py:15
  59.0 1.9 %copy-done = f32[2,2,2,2,2,128,256]{5,6,2,0,4,3,1:T(8,128)} copy-done((f32[2,2,2,2,2,128,256]{5,6,2,0,4,3,1:T(8,128)}, f32[2,2,2,2,2,128,256]{5,6,2,0,4,3,1:T(8,128)S(1)}, u32[]{:S(2)}) %copy-start) | copy-done | bytes 4194328
  60.9 2.0 %convert_bitcast_fusion.1 = bf16[2,2,2,2,2,128,256]{5,6,4,3,2,1,0:T(8,128)(2,1)S(1)} fusion(f32[2,2,2,2,2,128,256]{5,6,2,0,4,3,1:T(8,128)S(1)} %convolution_bitcast_fusion, f32[1,2,2,128,128]{4,3,2,1,0:T(8,128)S(1)} %slice.94, s32[]{:T(128)S(6)} %select_n.32), kind=kOutput, calls=%fused_computation.9 | convolution fusion | flops 806354944 | bytes 6356996 | tf_op jit(solution)/shard_map/nm,cdefgmx->cdefgnx/dot_general | solution.py:15
  63.0 2.4 %copy.160 = bf16[2,2,2,2,2,128,256]{6,5,4,3,2,1,0:T(8,128)(2,1)} copy(bf16[2,2,2,2,2,128,256]{5,6,4,3,2,1,0:T(8,128)(2,1)S(1)} %convert_bitcast_fusion.1) | data formatting | bytes 4194304 | tf_op jit(solution)/shard_map/convert_element_type | solution.py:126
  65.3 2.2 %copy.161 = bf16[2,2,16,2,2,8,2,2,128]{8,5,7,6,4,3,2,1,0:T(8,128)(2,1)S(1)} copy(bf16[2,2,16,2,2,8,2,2,128]{8,5,4,2,3,1,0,7,6:T(8,128)(2,1)} %bitcast.206) | data formatting | bytes 4194304 | tf_op jit(solution)/shard_map/transpose | solution.py:128
  67.5 5.4 %convert_bitcast_fusion = bf16[2,2,2,2,2,128,256]{5,6,4,3,2,1,0:T(8,128)(2,1)} fusion(f32[2,2,2,2,2,128,256]{5,6,2,0,4,3,1:T(8,128)} %copy-done, f32[1,2,2,128,128]{4,3,2,1,0:T(8,128)S(1)} %slice.94, s32[]{:T(128)S(6)} %select_n.36, s32[]{:T(128)S(6)} %select_n.32), kind=kOutput, calls=%fused_computation.8 | convolution fusion | flops 806354944 | bytes 6357000 | tf_op jit(solution)/shard_map/nm,cdefgmx->cdefgnx/dot_general | solution.py:15
  72.9 4.1 %copy.177 = bf16[2,2,2,2,2,128,256]{6,5,4,3,2,1,0:T(8,128)(2,1)} copy(bf16[2,2,2,2,2,128,256]{5,6,4,3,2,1,0:T(8,128)(2,1)} %convert_bitcast_fusion) | data formatting | bytes 4194304 | tf_op jit(solution)/shard_map/convert_element_type | solution.py:126
  77.0 3.5 %copy.178 = bf16[2,2,16,2,2,8,2,2,128]{8,5,7,6,4,3,2,1,0:T(8,128)(2,1)} copy(bf16[2,2,16,2,2,8,2,2,128]{8,5,4,2,3,1,0,7,6:T(8,128)(2,1)} %bitcast.207) | data formatting | bytes 4194304 | tf_op jit(solution)/shard_map/transpose | solution.py:128
  80.5 8.8 %collective-permute-start = (bf16[512,256]{1,0:T(8,128)(2,1)S(1)}, bf16[512,256]{1,0:T(8,128)(2,1)S(1)}, u32[]{:S(2)}, u32[]{:S(2)}) collective-permute-start(bf16[512,256]{1,0:T(8,128)(2,1)S(1)} %bitcast.216), channel_id=1, source_target_pairs={{0,64},{64,0},{1,65},{65,1},{2,66},{66,2},{3,67},{67,3},{4,68},{68... | collective-permute-start | bytes 786440 | tf_op jit(solution)/shard_map/ppermute | solution.py:113
  89.3 0.7 fusion.54
  90.0 22.7 %collective-permute-done = bf16[512,256]{1,0:T(8,128)(2,1)S(1)} collective-permute-done((bf16[512,256]{1,0:T(8,128)(2,1)S(1)}, bf16[512,256]{1,0:T(8,128)(2,1)S(1)}, u32[]{:S(2)}, u32[]{:S(2)}) %collective-permute-start) | collective-permute-done | bytes 262176 | tf_op jit(solution)/shard_map/ppermute | solution.py:113
  112.8 0.7 fusion.4
  113.5 34.9 %all_to_all.10 = bf16[64,32,256]{2,1,0:T(8,128)(2,1)S(1)} all-to-all(bf16[64,32,256]{2,1,0:T(8,128)(2,1)S(1)} %bitcast.210), channel_id=1, replica_groups=mesh['g'=4,'zh'=2,'zl'=4,'beam'=16] {'zl','beam'}, dimensions={0} | all-to-all | bytes 2097152 | tf_op jit(solution)/shard_map/all_to_all | solution.py:134
  148.4 0.6 copy.221
  149.0 1.1 reshape.109
  (55 shorter events, 1.5 us)
Async XLA Ops:
  0.0 5.0 %copy-start.2 = (f32[128,128,1]{1,0,2:T(8,128)S(1)}, f32[128,128,1]{1,0,2:T(8,128)}, u32[]{:S(2)}) copy-start(f32[128,128,1]{1,0,2:T(8,128)} %constant.123) | copy-start | bytes 196612
  0.0 4.4 %copy-start.7 = (f32[128,128,1]{1,0,2:T(8,128)S(1)}, f32[128,128,1]{1,0,2:T(8,128)}, u32[]{:S(2)}) copy-start(f32[128,128,1]{1,0,2:T(8,128)} %constant.124) | copy-start | bytes 196612
  0.0 4.6 %copy-start.8 = (f32[128,128]{1,0:T(8,128)S(1)}, f32[128,128]{1,0:T(8,128)}, u32[]{:S(2)}) copy-start(f32[128,128]{1,0:T(8,128)} %constant.114.clone) | copy-start | bytes 196612
  0.0 4.7 %copy-start.9 = (f32[128,128]{1,0:T(8,128)S(1)}, f32[128,128]{1,0:T(8,128)}, u32[]{:S(2)}) copy-start(f32[128,128]{1,0:T(8,128)} %constant.115.clone) | copy-start | bytes 196612
  4.7 1.1 copy-start.11
  5.5 1.2 copy-start.4
  6.1 1.2 copy-start.5
  6.1 1.2 copy-start.6
  6.7 1.4 copy-start.10
  13.5 1.8 %copy-start.3 = (f32[2,2,1,128,128]{4,3,2,1,0:T(8,128)S(1)}, f32[2,2,1,128,128]{4,3,2,1,0:T(8,128)}, u32[]{:S(2)}) copy-start(f32[2,2,1,128,128]{4,3,2,1,0:T(8,128)} %copy.172) | copy-start | bytes 786436
  15.2 14.6 %copy-start.12 = (s32[4,2,2,8]{3,2,1,0:T(2,128)S(1)}, s32[4,2,2,8]{3,2,1,0:T(2,128)}, u32[]{:S(2)}) copy-start(s32[4,2,2,8]{3,2,1,0:T(2,128)} %param.19) | copy-start | bytes 1540
  15.2 14.7 %copy-start.13 = (bf16[2,8,32]{2,1,0:T(8,128)(2,1)S(1)}, bf16[2,8,32]{2,1,0:T(8,128)(2,1)}, u32[]{:S(2)}) copy-start(bf16[2,8,32]{2,1,0:T(8,128)(2,1)} %param.16) | copy-start | bytes 3076
  15.2 39.9 %copy-start.14 = (f32[4,2,2,2]{0,3,2,1:T(2,128)S(1)}, f32[4,2,2,2]{0,3,2,1:T(2,128)}, u32[]{:S(2)}) copy-start(f32[4,2,2,2]{0,3,2,1:T(2,128)} %param.18) | copy-start | bytes 388
  16.8 63.7 %all-to-all-start = ((bf16[64,8,256]{2,1,0:T(8,128)(2,1)}), bf16[64,8,256]{2,1,0:T(8,128)(2,1)S(1)}, u32[]{:S(2)}, u32[]{:S(2)}) async-start(bf16[64,8,256]{2,1,0:T(8,128)(2,1)} %copy.175), calls=%async_computation | async-start | bytes 524288 | tf_op jit(solution)/shard_map/all_to_all | solution.py:112
  59.0 1.9 %copy-start = (f32[2,2,2,2,2,128,256]{5,6,2,0,4,3,1:T(8,128)}, f32[2,2,2,2,2,128,256]{5,6,2,0,4,3,1:T(8,128)S(1)}, u32[]{:S(2)}) copy-start(f32[2,2,2,2,2,128,256]{5,6,2,0,4,3,1:T(8,128)S(1)} %convolution_bitcast_fusion) | copy-start | bytes 12582916
  80.5 32.3 %collective-permute-start = (bf16[512,256]{1,0:T(8,128)(2,1)S(1)}, bf16[512,256]{1,0:T(8,128)(2,1)S(1)}, u32[]{:S(2)}, u32[]{:S(2)}) collective-permute-start(bf16[512,256]{1,0:T(8,128)(2,1)S(1)} %bitcast.216), channel_id=1, source_target_pairs={{0,64},{64,0},{1,65},{65,1},{2,66},{66,2},{3,67},{67,3},{4,68},{68... | collective-permute-start | bytes 786440 | tf_op jit(solution)/shard_map/ppermute | solution.py:113
  89.3 23.4 %copy-start.1 = (bf16[2,2,16,2,2,8,2,2,128]{8,5,7,6,4,3,2,1,0:T(8,128)(2,1)S(1)}, bf16[2,2,16,2,2,8,2,2,128]{8,5,7,6,4,3,2,1,0:T(8,128)(2,1)}, u32[]{:S(2)}) copy-start(bf16[2,2,16,2,2,8,2,2,128]{8,5,7,6,4,3,2,1,0:T(8,128)(2,1)} %copy.178) | copy-start | bytes 6291460
where the time goes:
time: 151 us; the launch traced here: 150 us
  blocking collectives  59.6 us (39%)
  waiting for transfers between devices  22.7 us (15%)
  local copies, waits for them, and re-layouts  22.1 us (15%)
  starting transfers between devices  21.9 us (15%)
  matrix products  20.8 us (14%)
  other arithmetic  2.36 us (2%)
    all_to_all x1, blocking collectives, local(): arrived = lax.all_to_all(result, ('zl', 'beam'), 0, 0, tiled=True)  34.9 us
    all_gather x1, blocking collectives, local(): packed = lax.all_gather(packed, 'beam', axis=0, tiled=True)  24.7 us
    ppermute x1, waiting for transfers between devices, local(): other = lax.ppermute(own, 'zh', [(0, 1), (1, 0)])  22.7 us
    dot_general x24, matrix products, table_product(): return jnp.einsum(form, left, right, precision=HIGH)  19.1 us
    all_to_all x1, starting transfers between devices, local(): lax.all_to_all(message, ('zl', 'beam'), 0, 0, tiled=True)  13.1 us
    ppermute x1, starting transfers between devices, local(): other = lax.ppermute(own, 'zh', [(0, 1), (1, 0)])  8.81 us
    convert_element_type x2, local copies, waits for them, and re-layouts, last(): full = table_product('nm,cdefgmx->cdefgnx', b4, lead).astype(jnp.bfloat16)  6.51 us
    transpose x2, local copies, waits for them, and re-layouts, last(): full = jnp.transpose(full, (2, 3, 5, 4, 7, 6, 0, 1, 8))  5.65 us
  transfers between devices with their start and end apart: 2, of which 1 were waited for; matrix products, arithmetic and copies ran while one was open for 16% of the time, Pallas kernels for 0%

commit v1 on v0

--- a/solution.py
+++ b/solution.py
@@ -99,7 +99,9 @@
         axis=1,
     )
     packed = jnp.pad(packed, ((0, 0), (0, 128 - packed.shape[1])))
-    packed = lax.all_gather(packed, "beam", axis=0, tiled=True)
+    packed = jnp.concatenate(
+        lax.all_to_all(jnp.stack([packed] * lax.axis_size("beam")), "beam", 0, 0), axis=0
+    )
     rows = packed.shape[0]
     compressed = compress(echoes, matched_filter)
     mats = range_chain(kernels, (zl & 1, zl >> 1, zh)).reshape(2, 2, FA, 2, FA)

time: 151 us -> 139 us (0.921)
  blocking collectives: 59.6 us -> 40.4 us
  starting transfers between devices: 21.9 us -> 29.1 us
  matrix products: 20.8 us -> 18.5 us
  local copies, waits for them, and re-layouts: 22.1 us -> 24 us
    all_gather x1 -> x0, blocking collectives: 24.7 us -> none  [local(): packed = lax.all_gather(packed, 'beam', axis=0, tiled=True)]
    all_to_all x0 -> x1, starting transfers between devices: none -> 10.1 us  [local(): lax.all_to_all(jnp.stack([packed] * lax.axis_size('beam')), 'beam', 0, 0)]
    all_to_all x1, blocking collectives: 34.9 us -> 40.4 us  [local(): arrived = lax.all_to_all(result, ('zl', 'beam'), 0, 0, tiled=True)]
    all_to_all x1, starting transfers between devices: 13.1 us -> 10.2 us  [local(): lax.all_to_all(message, ('zl', 'beam'), 0, 0, tiled=True)]
    dot_general x24, matrix products: 19.1 us -> 16.8 us  [table_product(): return jnp.einsum(form, left, right, precision=HIGH)]
  transfers between devices with their start and end apart: 2 -> 3, of which waited for: 1 -> 1; matrix products, arithmetic and copies ran while one was open for 16% -> 28% of each run, Pallas kernels for 0% -> 0%
where the time goes in v1:
time: 139 us; the launch traced here: 138 us
  blocking collectives  40.4 us (29%)
  starting transfers between devices  29.1 us (21%)
  local copies, waits for them, and re-layouts  24 us (17%)
  waiting for transfers between devices  22.2 us (16%)
  matrix products  18.5 us (13%)
  other arithmetic  3.09 us (2%)
    all_to_all x1, blocking collectives, local(): arrived = lax.all_to_all(result, ('zl', 'beam'), 0, 0, tiled=True)  40.4 us
    ppermute x1, waiting for transfers between devices, local(): other = lax.ppermute(own, 'zh', [(0, 1), (1, 0)])  22.2 us
    dot_general x24, matrix products, table_product(): return jnp.einsum(form, left, right, precision=HIGH)  16.8 us
    all_to_all x1, starting transfers between devices, local(): lax.all_to_all(message, ('zl', 'beam'), 0, 0, tiled=True)  10.2 us
    all_to_all x1, starting transfers between devices, local(): lax.all_to_all(jnp.stack([packed] * lax.axis_size('beam')), 'beam', 0, 0)  10.1 us
    ppermute x1, starting transfers between devices, local(): other = lax.ppermute(own, 'zh', [(0, 1), (1, 0)])  8.79 us
    convert_element_type x2, local copies, waits for them, and re-layouts, last(): full = table_product('nm,cdefgmx->cdefgnx', b4, lead).astype(jnp.bfloat16)  6.5 us
    transpose x2, local copies, waits for them, and re-layouts, last(): full = jnp.transpose(full, (2, 3, 5, 4, 7, 6, 0, 1, 8))  5.8 us
  transfers between devices with their start and end apart: 3, of which 1 were waited for; matrix products, arithmetic and copies ran while one was open for 28% of the time, Pallas kernels for 0%

profile of v1, /device:TPU:1, one launch (start us, length us, event | category | flops | bytes accessed | tf_op | source)
XLA Modules:
  0.0 137.9 jit_solution(13612512444076500274)
XLA Ops:
  0.0 0.7 convert_element_type.52
  0.9 0.7 copy.122
  1.7 0.6 stack.18
  2.3 10.1 %all-to-all-start = ((bf16[16,8,128]{2,1,0:T(8,128)(2,1)}), bf16[16,8,128]{2,1,0:T(8,128)(2,1)S(1)}, u32[]{:S(2)}, u32[]{:S(2)}) async-start(bf16[16,8,128]{2,1,0:T(8,128)(2,1)} %stack.18), calls=%async_computation | async-start | bytes 65536 | tf_op jit(solution)/shard_map/all_to_all | solution.py:103
  12.5 1.2 reshape.134
  13.6 1.1 fusion.34
  14.7 1.1 fusion.33
  15.7 1.1 convolution_add_fusion.4
  17.1 0.3 fusion.20
  17.6 0.3 fusion.13
  17.9 0.3 fusion.14
  18.5 0.3 fusion.43
  18.8 0.3 fusion.44
  19.1 0.3 fusion.12
  19.4 0.3 fusion.11
  19.7 0.4 fusion.36
  20.1 0.4 fusion.35
  20.6 0.9 slice_bitcast_fusion.2
  21.5 0.4 convolution_subtract_fusion
  22.1 0.4 convolution_add_fusion.1
  22.5 0.8 copy.144
  23.3 1.4 %maximum_maximum_fusion = f32[4,2,256,256]{3,2,1,0:T(8,128)S(1)} fusion(f32[4,2,128,128]{3,2,1,0:T(8,128)} %get-tuple-element.9, f32[4,2,128,128]{3,2,1,0:T(8,128)S(1)} %fusion.58, f32[4,2,128,128]{3,2,1,0:T(8,128)S(1)} %get-tuple-element.8), kind=kLoop, calls=%fused_computation.7 | loop fusion | flops 1572864 | bytes 3670016 | tf_op jit(solution)/shard_map/concatenate | solution.py:63
  24.7 1.0 fusion.59
  25.7 0.3 fusion.25
  25.9 1.3 convolution_bitcast_fusion.3
  27.2 0.4 convolution_convert_fusion
  27.7 0.3 fusion.10
  28.3 0.9 copy.147
  29.3 10.2 %all-to-all-start.1 = ((bf16[64,8,256]{2,1,0:T(8,128)(2,1)}), bf16[64,8,256]{2,1,0:T(8,128)(2,1)S(1)}, u32[]{:S(2)}, u32[]{:S(2)}) async-start(bf16[64,8,256]{2,1,0:T(8,128)(2,1)} %copy.147), calls=%async_computation.1 | async-start | bytes 524288 | tf_op jit(solution)/shard_map/all_to_all | solution.py:114
  39.8 0.6 select_add_fusion
  40.5 0.3 convolution_bitcast_fusion.4
  41.0 0.6 convolution_bitcast_fusion.1
  41.6 1.9 %convolution_bitcast_fusion = f32[2,2,2,2,2,128,256]{5,6,2,0,4,3,1:T(8,128)S(1)} fusion(f32[2,2,2,128,256,1,1]{3,4,6,5,2,1,0:T(8,128)S(1)} %convolution_bitcast_fusion.1, f32[4,2,2,128,128]{4,3,2,1,0:T(8,128)S(1)} %select_add_fusion), kind=kOutput, calls=%fused_computation.6 | convolution fusion | flops 805306368 | bytes 5505024 | tf_op jit(solution)/shard_map/cenm,dfgmx->cdefgnx/dot_general | solution.py:15
  43.5 1.9 %copy-done = f32[2,2,2,2,2,128,256]{5,6,2,0,4,3,1:T(8,128)} copy-done((f32[2,2,2,2,2,128,256]{5,6,2,0,4,3,1:T(8,128)}, f32[2,2,2,2,2,128,256]{5,6,2,0,4,3,1:T(8,128)S(1)}, u32[]{:S(2)}) %copy-start) | copy-done | bytes 4194328
  45.4 2.0 %convert_bitcast_fusion.1 = bf16[2,2,2,2,2,128,256]{5,6,4,3,2,1,0:T(8,128)(2,1)S(1)} fusion(f32[2,2,2,2,2,128,256]{5,6,2,0,4,3,1:T(8,128)S(1)} %convolution_bitcast_fusion, f32[1,2,2,128,128]{4,3,2,1,0:T(8,128)S(1)} %slice.94, s32[]{:T(128)S(6)} %select_n.32), kind=kOutput, calls=%fused_computation.9 | convolution fusion | flops 806354944 | bytes 6356996 | tf_op jit(solution)/shard_map/nm,cdefgmx->cdefgnx/dot_general | solution.py:15
  47.4 2.4 %copy.132 = bf16[2,2,2,2,2,128,256]{6,5,4,3,2,1,0:T(8,128)(2,1)} copy(bf16[2,2,2,2,2,128,256]{5,6,4,3,2,1,0:T(8,128)(2,1)S(1)} %convert_bitcast_fusion.1) | data formatting | bytes 4194304 | tf_op jit(solution)/shard_map/convert_element_type | solution.py:128
  49.8 2.3 %copy.133 = bf16[2,2,16,2,2,8,2,2,128]{8,5,7,6,4,3,2,1,0:T(8,128)(2,1)S(1)} copy(bf16[2,2,16,2,2,8,2,2,128]{8,5,4,2,3,1,0,7,6:T(8,128)(2,1)} %bitcast.207) | data formatting | bytes 4194304 | tf_op jit(solution)/shard_map/transpose | solution.py:130
  52.1 0.5 copy-done.1
  52.6 3.1 %convert_bitcast_fusion = bf16[2,2,2,2,2,128,256]{5,6,4,3,2,1,0:T(8,128)(2,1)} fusion(f32[2,2,2,2,2,128,256]{5,6,2,0,4,3,1:T(8,128)S(1)} %copy-done.1, f32[1,2,2,128,128]{4,3,2,1,0:T(8,128)S(1)} %slice.94, s32[]{:T(128)S(6)} %select_n.36, s32[]{:T(128)S(6)} %select_n.32), kind=kOutput, calls=%fused_computation.8 | convolution fusion | flops 806354944 | bytes 6357000 | tf_op jit(solution)/shard_map/nm,cdefgmx->cdefgnx/dot_general | solution.py:15
  55.7 4.1 %copy.149 = bf16[2,2,2,2,2,128,256]{6,5,4,3,2,1,0:T(8,128)(2,1)} copy(bf16[2,2,2,2,2,128,256]{5,6,4,3,2,1,0:T(8,128)(2,1)} %convert_bitcast_fusion) | data formatting | bytes 4194304 | tf_op jit(solution)/shard_map/convert_element_type | solution.py:128
  59.8 3.5 %copy.150 = bf16[2,2,16,2,2,8,2,2,128]{8,5,7,6,4,3,2,1,0:T(8,128)(2,1)} copy(bf16[2,2,16,2,2,8,2,2,128]{8,5,4,2,3,1,0,7,6:T(8,128)(2,1)} %bitcast.208) | data formatting | bytes 4194304 | tf_op jit(solution)/shard_map/transpose | solution.py:130
  63.3 8.8 %collective-permute-start = (bf16[512,256]{1,0:T(8,128)(2,1)S(1)}, bf16[512,256]{1,0:T(8,128)(2,1)S(1)}, u32[]{:S(2)}, u32[]{:S(2)}) collective-permute-start(bf16[512,256]{1,0:T(8,128)(2,1)S(1)} %bitcast.217), channel_id=1, source_target_pairs={{0,64},{64,0},{1,65},{65,1},{2,66},{66,2},{3,67},{67,3},{4,68},{68... | collective-permute-start | bytes 786440 | tf_op jit(solution)/shard_map/ppermute | solution.py:115
  72.1 0.7 fusion.54
  72.8 22.2 %collective-permute-done = bf16[512,256]{1,0:T(8,128)(2,1)S(1)} collective-permute-done((bf16[512,256]{1,0:T(8,128)(2,1)S(1)}, bf16[512,256]{1,0:T(8,128)(2,1)S(1)}, u32[]{:S(2)}, u32[]{:S(2)}) %collective-permute-start) | collective-permute-done | bytes 262176 | tf_op jit(solution)/shard_map/ppermute | solution.py:115
  95.0 0.7 fusion.4
  95.7 40.4 %all_to_all.15 = bf16[64,32,256]{2,1,0:T(8,128)(2,1)S(1)} all-to-all(bf16[64,32,256]{2,1,0:T(8,128)(2,1)S(1)} %bitcast.211), channel_id=1, replica_groups=mesh['g'=4,'zh'=2,'zl'=4,'beam'=16] {'zl','beam'}, dimensions={0} | all-to-all | bytes 2097152 | tf_op jit(solution)/shard_map/all_to_all | solution.py:136
  136.2 0.6 copy.193
  136.8 1.1 reshape.115
  (55 shorter events, 2.4 us)
Async XLA Ops:
  0.0 17.3 %copy-start.3 = (f32[128,128,1]{1,0,2:T(8,128)S(1)}, f32[128,128,1]{1,0,2:T(8,128)}, u32[]{:S(2)}) copy-start(f32[128,128,1]{1,0,2:T(8,128)} %constant.123) | copy-start | bytes 196612
  0.0 16.8 %copy-start.8 = (f32[128,128,1]{1,0,2:T(8,128)S(1)}, f32[128,128,1]{1,0,2:T(8,128)}, u32[]{:S(2)}) copy-start(f32[128,128,1]{1,0,2:T(8,128)} %constant.124) | copy-start | bytes 196612
  0.0 17.0 %copy-start.9 = (f32[128,128]{1,0:T(8,128)S(1)}, f32[128,128]{1,0:T(8,128)}, u32[]{:S(2)}) copy-start(f32[128,128]{1,0:T(8,128)} %constant.114.clone) | copy-start | bytes 196612
  0.0 17.0 %copy-start.10 = (f32[128,128]{1,0:T(8,128)S(1)}, f32[128,128]{1,0:T(8,128)}, u32[]{:S(2)}) copy-start(f32[128,128]{1,0:T(8,128)} %constant.115.clone) | copy-start | bytes 196612
  2.3 27.0 %all-to-all-start = ((bf16[16,8,128]{2,1,0:T(8,128)(2,1)}), bf16[16,8,128]{2,1,0:T(8,128)(2,1)S(1)}, u32[]{:S(2)}, u32[]{:S(2)}) async-start(bf16[16,8,128]{2,1,0:T(8,128)(2,1)} %stack.18), calls=%async_computation | async-start | bytes 65536 | tf_op jit(solution)/shard_map/all_to_all | solution.py:103
  17.1 1.1 copy-start.12
  17.9 1.2 copy-start.5
  18.5 1.2 copy-start.6
  18.5 1.2 copy-start.7
  19.1 1.4 %copy-start.11 = (bf16[4,2,2,128,128]{4,3,2,1,0:T(8,128)(2,1)S(1)}, bf16[4,2,2,128,128]{4,3,2,1,0:T(8,128)(2,1)}, u32[]{:S(2)}) copy-start(bf16[4,2,2,128,128]{4,3,2,1,0:T(8,128)(2,1)} %param.17) | copy-start | bytes 1572868
  25.7 2.3 %copy-start.13 = (f32[4,2,2,2]{0,3,2,1:T(2,128)S(1)}, f32[4,2,2,2]{0,3,2,1:T(2,128)}, u32[]{:S(2)}) copy-start(f32[4,2,2,2]{0,3,2,1:T(2,128)} %param.18) | copy-start | bytes 388
  25.9 1.7 %copy-start.4 = (f32[2,2,1,128,128]{4,3,2,1,0:T(8,128)S(1)}, f32[2,2,1,128,128]{4,3,2,1,0:T(8,128)}, u32[]{:S(2)}) copy-start(f32[2,2,1,128,128]{4,3,2,1,0:T(8,128)} %copy.144) | copy-start | bytes 786436
  29.3 34.0 %all-to-all-start.1 = ((bf16[64,8,256]{2,1,0:T(8,128)(2,1)}), bf16[64,8,256]{2,1,0:T(8,128)(2,1)S(1)}, u32[]{:S(2)}, u32[]{:S(2)}) async-start(bf16[64,8,256]{2,1,0:T(8,128)(2,1)} %copy.147), calls=%async_computation.1 | async-start | bytes 524288 | tf_op jit(solution)/shard_map/all_to_all | solution.py:114
  43.5 1.9 %copy-start = (f32[2,2,2,2,2,128,256]{5,6,2,0,4,3,1:T(8,128)}, f32[2,2,2,2,2,128,256]{5,6,2,0,4,3,1:T(8,128)S(1)}, u32[]{:S(2)}) copy-start(f32[2,2,2,2,2,128,256]{5,6,2,0,4,3,1:T(8,128)S(1)} %convolution_bitcast_fusion) | copy-start | bytes 12582916
  49.8 2.8 %copy-start.1 = (f32[2,2,2,2,2,128,256]{5,6,2,0,4,3,1:T(8,128)S(1)}, f32[2,2,2,2,2,128,256]{5,6,2,0,4,3,1:T(8,128)}, u32[]{:S(2)}) copy-start(f32[2,2,2,2,2,128,256]{5,6,2,0,4,3,1:T(8,128)} %copy-done) | copy-start | bytes 12582916
  63.3 31.7 %collective-permute-start = (bf16[512,256]{1,0:T(8,128)(2,1)S(1)}, bf16[512,256]{1,0:T(8,128)(2,1)S(1)}, u32[]{:S(2)}, u32[]{:S(2)}) collective-permute-start(bf16[512,256]{1,0:T(8,128)(2,1)S(1)} %bitcast.217), channel_id=1, source_target_pairs={{0,64},{64,0},{1,65},{65,1},{2,66},{66,2},{3,67},{67,3},{4,68},{68... | collective-permute-start | bytes 786440 | tf_op jit(solution)/shard_map/ppermute | solution.py:115
  72.1 22.9 %copy-start.2 = (bf16[2,2,16,2,2,8,2,2,128]{8,5,7,6,4,3,2,1,0:T(8,128)(2,1)S(1)}, bf16[2,2,16,2,2,8,2,2,128]{8,5,7,6,4,3,2,1,0:T(8,128)(2,1)}, u32[]{:S(2)}) copy-start(bf16[2,2,16,2,2,8,2,2,128]{8,5,7,6,4,3,2,1,0:T(8,128)(2,1)} %copy.150) | copy-start | bytes 6291460
